TPU v7x, 32 devices: a whole 2x2x4 slice. The times are simulated.
32 devices in a mesh: rep: 8 (over y, x, core), shard: 4 (over z).
Axes of the slice: x: 2, y: 2, z: 4, core: 2. Of those that a mesh axis runs over, the one named last changes fastest.
Arguments:
- tokens: bfloat16 [4, 1024, 2048], P('shard', 'rep'), may hold values from -6 to 6
- teacher: bfloat16 [4, 1024, 2048], P('shard', 'rep'), may hold values from -6 to 6
- valid_mask: int32 [4, 1024], P('shard', 'rep'), may hold values from 0 to 1, as said below
- block_mask: int32 [4, 4, 4], P('shard'), may hold values 0 or 1
- routes: int32 [4, 1024, 4], P('shard', 'rep'), may hold values from 0 to 7, all different within a row; in each aligned block of 128 rows (0 to 127, 128 to 255, ..., all dimensions but the last counted through in order) at most 80 rows name the same one
- gates: float32 [4, 1024, 4], P('shard', 'rep'), may hold values from 0.3 to 1
- attn_gain: bfloat16 [2048], P('shard'), may hold values from 0.5 to 1.5
- w_qkv: bfloat16 [3, 2048, 2048], P(None, 'shard'), may hold values from -0.21875 to 0.21875
- qkv_bias: bfloat16 [3, 2048], P(None, 'shard'), may hold values from -3 to 3
- w_out: bfloat16 [2048, 2048], P('shard'), may hold values from -0.375 to 0.375
- ffn_gain: bfloat16 [2048], P('shard'), may hold values from 0.5 to 1.5
- shared_gate_up: bfloat16 [2, 2048, 5632], P(None, 'shard'), may hold values from -0.125 to 0.125
- shared_down: bfloat16 [5632, 2048], P('shard'), may hold values from -0.078125 to 0.078125
- shared_gate: bfloat16 [2048], P('shard'), may hold values from -0.125 to 0.125
- expert_gate_up: bfloat16 [8, 2, 2048, 1408], P('shard'), may hold values from -0.125 to 0.125
- expert_down: bfloat16 [8, 1408, 2048], P('shard'), may hold values from -0.15625 to 0.15625
Outputs:
- loss: float32 [], replicated
- block_out: bfloat16 [4, 1024, 2048], P('shard', 'rep')
- input_grad: float32 [4, 1024, 2048], P('shard', 'rep')
- attn_gain_grad: float32 [2048], P('shard')
- w_qkv_grad: float32 [3, 2048, 2048], P(None, 'shard', 'rep')
- qkv_bias_grad: float32 [3, 2048], P(None, 'shard')
- w_out_grad: float32 [2048, 2048], P('shard', 'rep')
- ffn_gain_grad: float32 [2048], P('shard')
- shared_gate_up_grad: float32 [2, 2048, 5632], P(None, 'shard', 'rep')
- shared_down_grad: float32 [5632, 2048], P('shard', 'rep')
- shared_gate_grad: float32 [2048], P('shard')
- expert_gate_up_grad: float32 [8, 2, 2048, 1408], P('shard', None, 'rep')
- expert_down_grad: float32 [8, 1408, 2048], P('shard', None, 'rep')
Inputs may be any that keep to these rules, and one draw needn't show every extreme that they name: `routes`: each row names 4 different experts; in the 128 rows of one device no expert is named by more than 80 rows, a bound that some block reaches. `valid_mask`: 1 at every position of a sequence that is a multiple of 256.
All inputs are finite; a program needn't handle non-finite values. No bound on the sum of `block_mask` on one device may be relied on, other than what follows from the above.
Results may differ from a plain program's by a relative error of at most 0.025.
Values may be sent and summed in bfloat16 or wider, within the bound.
A program may use at most 704 MiB of HBM per device.

v0:
```python
import math

import jax
import jax.numpy as jnp
from jax import lax
from jax.sharding import PartitionSpec as P

HEADS = 16
HD = 128
BLOCK = 256
CAP = 80


EPS = 1e-06
THETA = 1000000.0
NEG = -1e30
KEY_SPAN = 1024


def norm_scale(values):
    return lax.rsqrt(jnp.mean(values * values, axis=-1, keepdims=True) + EPS)


def norm_back(values, gain_vec, grad_out):
    scaling = norm_scale(values)
    normed = values * scaling
    d_normed = grad_out * gain_vec
    d_gain = jnp.sum(grad_out * normed, axis=0)
    d_values = scaling * (d_normed - normed * jnp.mean(d_normed * normed, axis=-1, keepdims=True))
    return (d_values, d_gain)


def rope_tables(offset, count, width):
    half_width = width // 2
    feature = jnp.arange(half_width, dtype=jnp.int32).astype(jnp.float32)
    frequency = THETA ** (-2.0 * feature / width)
    places = (offset + jnp.arange(count, dtype=jnp.int32)).astype(jnp.float32)
    angles = places[:, None] * frequency[None, :]
    angles = jnp.concatenate([angles, angles], axis=1)
    return (jnp.cos(angles), jnp.sin(angles))


def rotate(values, cosine_table, sine_table, head_count):
    row_count = values.shape[0]
    shaped = values.reshape(row_count, head_count, -1)
    half_width = shaped.shape[-1] // 2
    turned = jnp.concatenate([-shaped[..., half_width:], shaped[..., :half_width]], axis=-1)
    return (shaped * cosine_table[:, None, :] + turned * sine_table[:, None, :]).reshape(
        row_count, -1
    )


def rotate_back(gradient, cosine_table, sine_table, head_count):
    row_count = gradient.shape[0]
    shaped = gradient.reshape(row_count, head_count, -1)
    half_width = shaped.shape[-1] // 2
    sine_part = shaped * sine_table[:, None, :]
    turned = jnp.concatenate([sine_part[..., half_width:], -sine_part[..., :half_width]], axis=-1)
    return (shaped * cosine_table[:, None, :] + turned).reshape(row_count, -1)


def swiglu(gate_part, up_part):
    return jax.nn.silu(gate_part) * up_part


def swiglu_grads(gate_part, up_part, d_hidden):
    sigmoid_val = jax.nn.sigmoid(gate_part)
    d_gate = d_hidden * up_part * sigmoid_val * (1.0 + gate_part * (1.0 - sigmoid_val))
    d_up_part = d_hidden * gate_part * sigmoid_val
    return (d_gate, d_up_part)


def keep_state(carried):
    return carried


def allowed_keys(block_table, query_first, query_count, key_first, key_count, block_len):
    query_blocks = (query_first + jnp.arange(query_count, dtype=jnp.int32)) // block_len
    key_blocks = (key_first + jnp.arange(key_count, dtype=jnp.int32)) // block_len
    table_rows = jnp.take(block_table, query_blocks, axis=0)
    chosen = jnp.take(table_rows, key_blocks, axis=1)
    earlier = (key_blocks[None, :] < query_blocks[:, None]) & (chosen == 1)
    return earlier | (key_blocks[None, :] == query_blocks[:, None])


def expert_forward(inputs, gate_up_weight, down_weight):
    pre_act = jnp.einsum(
        "sgcd,gjdf->sgcjf", inputs, gate_up_weight, preferred_element_type=jnp.float32
    )
    hidden = swiglu(pre_act[..., 0, :], pre_act[..., 1, :]).astype(jnp.bfloat16)
    outputs = jnp.einsum("sgcf,gfd->sgcd", hidden, down_weight, preferred_element_type=jnp.float32)
    return (outputs.astype(jnp.bfloat16), pre_act)


def expert_input_grads(pre_act, d_outputs, gate_up_weight, down_weight):
    d_hidden = jnp.einsum(
        "sgcd,gfd->sgcf", d_outputs, down_weight, preferred_element_type=jnp.float32
    )
    d_gate, d_up_part = swiglu_grads(pre_act[..., 0, :], pre_act[..., 1, :], d_hidden)
    d_pre = jnp.stack([d_gate, d_up_part], axis=-2).astype(jnp.bfloat16)
    d_inputs = jnp.einsum(
        "sgcjf,gjdf->sgcd", d_pre, gate_up_weight, preferred_element_type=jnp.float32
    )
    return (d_inputs.astype(jnp.bfloat16), d_pre)


def expert_weight_grads(inputs, pre_act, d_pre, d_outputs):
    hidden = swiglu(pre_act[..., 0, :], pre_act[..., 1, :]).astype(jnp.bfloat16)
    d_gate_up = jnp.einsum("sgcd,sgcjf->gjdf", inputs, d_pre, preferred_element_type=jnp.float32)
    d_down = jnp.einsum("sgcf,sgcd->gfd", hidden, d_outputs, preferred_element_type=jnp.float32)
    return (d_gate_up, d_down)


def per_device(
    tokens,
    teacher,
    valid_mask,
    block_mask,
    routes,
    gates,
    attn_gain,
    w_qkv,
    qkv_bias,
    w_out,
    ffn_gain,
    shared_gate_up,
    shared_down,
    shared_gate,
    expert_gate_up,
    expert_down,
):
    x_rows = tokens[0].astype(jnp.float32)
    row_count = x_rows.shape[0]
    model_width = x_rows.shape[1]
    groups = lax.axis_size("shard")
    replicas = lax.axis_size("rep")
    local_experts = expert_gate_up.shape[0]
    experts_total = groups * local_experts
    first_row = lax.axis_index("rep") * row_count
    last_row = first_row + row_count - 1
    seq_len = row_count * replicas
    key_len = min(KEY_SPAN, seq_len)
    key_count = seq_len // key_len
    score_scale = 1.0 / math.sqrt(HD)
    block_table = block_mask[0]
    attn_gain_all, qkv_all, bias_all, out_weight_all = (
        lax.all_gather(attn_gain, "shard", axis=0, tiled=True),
        lax.all_gather(w_qkv, "shard", axis=1, tiled=True),
        lax.all_gather(qkv_bias, "shard", axis=1, tiled=True),
        lax.all_gather(w_out, "shard", axis=0, tiled=True),
    )
    attn_gain_float = attn_gain_all.astype(jnp.float32)
    normed_low = (x_rows * norm_scale(x_rows) * attn_gain_float).astype(jnp.bfloat16)
    projected = jnp.einsum("ld,jdf->jlf", normed_low, qkv_all, preferred_element_type=jnp.float32)
    projected = projected + bias_all.astype(jnp.float32)[:, None, :]
    cosine_table, sine_table = rope_tables(first_row, row_count, HD)
    query_low = rotate(projected[0], cosine_table, sine_table, HEADS).astype(jnp.bfloat16)
    key_low = rotate(projected[1], cosine_table, sine_table, HEADS).astype(jnp.bfloat16)
    value_low = projected[2].astype(jnp.bfloat16)
    all_keys, all_values = (
        lax.all_gather(key_low, "rep", axis=0, tiled=True),
        lax.all_gather(value_low, "rep", axis=0, tiled=True),
    )
    query_heads = query_low.reshape(row_count, HEADS, HD)

    def block_scores(block_index):
        key_first = block_index * key_len
        key_part = lax.dynamic_slice_in_dim(all_keys, key_first, key_len, 0).reshape(
            key_len, HEADS, HD
        )
        value_part = lax.dynamic_slice_in_dim(all_values, key_first, key_len, 0).reshape(
            key_len, HEADS, HD
        )
        raw_scores = (
            jnp.einsum("qhd,khd->hqk", query_heads, key_part, preferred_element_type=jnp.float32)
            * score_scale
        )
        permitted = allowed_keys(block_table, first_row, row_count, key_first, key_len, BLOCK)[None]
        masked = jnp.where(permitted, raw_scores, NEG)
        return (masked, permitted, key_part, value_part)

    def lse_step(block_index, carried):

        def lse_live_block(running):
            run_max, run_total = running
            masked, permitted, key_part, value_part = block_scores(block_index)
            new_max = jnp.maximum(run_max, jnp.max(masked, axis=-1))
            weights = jnp.where(permitted, jnp.exp(masked - new_max[..., None]), 0.0)
            return (new_max, run_total * jnp.exp(run_max - new_max) + jnp.sum(weights, axis=-1))

        return lax.cond(block_index * key_len <= last_row, lse_live_block, keep_state, carried)

    start_stats = (
        jnp.full((HEADS, row_count), NEG, jnp.float32),
        jnp.zeros((HEADS, row_count), jnp.float32),
    )
    run_max, run_total = lax.fori_loop(0, key_count, lse_step, start_stats)
    log_total = run_max + jnp.log(run_total)

    def probs_of(masked, permitted):
        return jnp.where(permitted, jnp.exp(masked - log_total[..., None]), 0.0)

    def output_step(block_index, partial_out):

        def output_live_block(running):
            masked, permitted, key_part, value_part = block_scores(block_index)
            weights_low = probs_of(masked, permitted).astype(jnp.bfloat16)
            return running + jnp.einsum(
                "hqk,khd->qhd", weights_low, value_part, preferred_element_type=jnp.float32
            )

        return lax.cond(
            block_index * key_len <= last_row, output_live_block, keep_state, partial_out
        )

    attended = lax.fori_loop(
        0, key_count, output_step, jnp.zeros((row_count, HEADS, HD), jnp.float32)
    )
    attended_low = attended.reshape(row_count, HEADS * HD).astype(jnp.bfloat16)
    mid_rows = x_rows + jnp.dot(attended_low, out_weight_all, preferred_element_type=jnp.float32)
    ffn_gain_all, shared_gate_up_all, shared_down_all, shared_gate_all = (
        lax.all_gather(ffn_gain, "shard", axis=0, tiled=True),
        lax.all_gather(shared_gate_up, "shard", axis=1, tiled=True),
        lax.all_gather(shared_down, "shard", axis=0, tiled=True),
        lax.all_gather(shared_gate, "shard", axis=0, tiled=True),
    )
    ffn_gain_float = ffn_gain_all.astype(jnp.float32)
    normed_mid = (mid_rows * norm_scale(mid_rows) * ffn_gain_float).astype(jnp.bfloat16)
    shared_pre = jnp.einsum(
        "ld,jdf->jlf", normed_mid, shared_gate_up_all, preferred_element_type=jnp.float32
    )
    shared_hidden = swiglu(shared_pre[0], shared_pre[1]).astype(jnp.bfloat16)
    shared_out = jnp.dot(shared_hidden, shared_down_all, preferred_element_type=jnp.float32)
    shared_weight = jax.nn.sigmoid(
        jnp.dot(normed_mid, shared_gate_all, preferred_element_type=jnp.float32)
    )
    route_rows = routes[0]
    gate_rows = gates[0]
    top_count = route_rows.shape[1]
    flat_expert = route_rows.reshape(-1)
    one_hot = (flat_expert[:, None] == jnp.arange(experts_total, dtype=jnp.int32)[None, :]).astype(
        jnp.int32
    )
    flat_slot = jnp.sum((jnp.cumsum(one_hot, axis=0) - one_hot) * one_hot, axis=1)
    flat_token = jnp.arange(row_count * top_count, dtype=jnp.int32) // top_count
    slot_token = (
        jnp.zeros((experts_total, CAP), jnp.int32).at[flat_expert, flat_slot].set(flat_token)
    )
    token_buffer = normed_mid[slot_token]
    received = lax.all_to_all(token_buffer, "shard", split_axis=0, concat_axis=0, tiled=True)
    shaped = received.reshape(groups, local_experts, received.shape[1], received.shape[2])
    outputs, pre_act = expert_forward(shaped, expert_gate_up, expert_down)
    sent_out = outputs.reshape(received.shape)
    pre_remote = pre_act.reshape(received.shape[0], received.shape[1], 2, -1)
    expert_buffer = lax.all_to_all(sent_out, "shard", split_axis=0, concat_axis=0, tiled=True)
    picked = expert_buffer[flat_expert, flat_slot].reshape(row_count, top_count, model_width)
    expert_mix = jnp.sum(gate_rows[:, :, None] * picked.astype(jnp.float32), axis=1)
    out_rows = mid_rows + shared_weight[:, None] * shared_out + expert_mix
    diff_rows = out_rows - teacher[0].astype(jnp.float32)
    valid_rows = valid_mask[0].astype(jnp.float32)
    squares_local = jnp.sum(valid_rows * jnp.sum(diff_rows * diff_rows, axis=1))
    count_local = jnp.sum(valid_rows)
    squares_total, count_total = lax.psum((squares_local, count_local), ("rep", "shard"))
    loss_value = squares_total / (count_total * model_width)
    tokens_all = row_count * replicas * groups
    d_rows = valid_rows[:, None] * diff_rows * (tokens_all / (2.0 * count_total))
    d_shared_out = (shared_weight[:, None] * d_rows).astype(jnp.bfloat16)
    d_shared_hidden = jnp.einsum(
        "ld,fd->lf", d_shared_out, shared_down_all, preferred_element_type=jnp.float32
    )
    d_shared_down = jnp.einsum(
        "lf,ld->fd", shared_hidden, d_shared_out, preferred_element_type=jnp.float32
    )
    d_logit = jnp.sum(shared_out * d_rows, axis=1) * shared_weight * (1.0 - shared_weight)
    d_shared_gate = jnp.einsum("l,ld->d", d_logit, normed_mid.astype(jnp.float32))
    d_gate_shared, d_up_shared = swiglu_grads(shared_pre[0], shared_pre[1], d_shared_hidden)
    d_shared_pre = jnp.stack([d_gate_shared, d_up_shared]).astype(jnp.bfloat16)
    d_shared_gate_up = jnp.einsum(
        "ld,jlf->jdf", normed_mid, d_shared_pre, preferred_element_type=jnp.float32
    )
    d_normed_mid = jnp.einsum(
        "jlf,jdf->ld", d_shared_pre, shared_gate_up_all, preferred_element_type=jnp.float32
    )
    d_normed_mid = d_normed_mid + d_logit[:, None] * shared_gate_all.astype(jnp.float32)[None, :]
    d_picked = (gate_rows[:, :, None] * d_rows[:, None, :]).astype(jnp.bfloat16)
    d_picked = d_picked.reshape(row_count * top_count, model_width)
    d_buffer = (
        jnp.zeros((experts_total, CAP, model_width), jnp.bfloat16)
        .at[flat_expert, flat_slot]
        .set(d_picked)
    )
    d_remote = lax.all_to_all(d_buffer, "shard", split_axis=0, concat_axis=0, tiled=True)
    lead_shape = (groups, local_experts, d_remote.shape[1])
    pre_shaped = pre_remote.reshape(lead_shape + pre_remote.shape[2:])
    d_shaped = d_remote.reshape(lead_shape + d_remote.shape[2:])
    d_inputs_remote, d_pre_remote = expert_input_grads(
        pre_shaped, d_shaped, expert_gate_up, expert_down
    )
    d_token_buffer = lax.all_to_all(
        d_inputs_remote.reshape(d_remote.shape), "shard", split_axis=0, concat_axis=0, tiled=True
    )
    inputs_shaped = received.reshape(lead_shape + received.shape[2:])
    d_expert_gate_up, d_expert_down = expert_weight_grads(
        inputs_shaped, pre_shaped, d_pre_remote, d_shaped
    )
    d_from_experts = d_token_buffer[flat_expert, flat_slot].astype(jnp.float32)
    d_from_experts = jnp.sum(d_from_experts.reshape(row_count, top_count, model_width), axis=1)
    d_normed_mid = d_normed_mid + d_from_experts
    d_mid_norm, d_ffn_gain = norm_back(mid_rows, ffn_gain_float, d_normed_mid)
    d_mid = d_rows + d_mid_norm
    d_branch = d_mid.astype(jnp.bfloat16)
    d_out_weight = jnp.einsum(
        "lf,ld->fd", attended_low, d_branch, preferred_element_type=jnp.float32
    )
    d_attended = jnp.einsum(
        "ld,fd->lf", d_branch, out_weight_all, preferred_element_type=jnp.float32
    )
    d_attended = d_attended.astype(jnp.bfloat16).reshape(row_count, HEADS, HD)
    delta_rows = jnp.einsum("qhd,qhd->hq", d_attended.astype(jnp.float32), attended)

    def grad_step(block_index, carried):

        def grad_live_block(running):
            d_query, d_keys, d_values = running
            key_first = block_index * key_len
            masked, permitted, key_part, value_part = block_scores(block_index)
            weights_full = probs_of(masked, permitted)
            d_value_part = jnp.einsum(
                "hqk,qhd->khd",
                weights_full.astype(jnp.bfloat16),
                d_attended,
                preferred_element_type=jnp.float32,
            )
            d_weights = jnp.einsum(
                "qhd,khd->hqk", d_attended, value_part, preferred_element_type=jnp.float32
            )
            d_scores = (weights_full * (d_weights - delta_rows[..., None])).astype(jnp.bfloat16)
            d_query = d_query + jnp.einsum(
                "hqk,khd->qhd", d_scores, key_part, preferred_element_type=jnp.float32
            )
            d_key_part = (
                jnp.einsum(
                    "hqk,qhd->khd", d_scores, query_heads, preferred_element_type=jnp.float32
                )
                * score_scale
            )
            d_keys = lax.dynamic_update_slice_in_dim(
                d_keys, d_key_part.reshape(key_len, -1), key_first, 0
            )
            d_values = lax.dynamic_update_slice_in_dim(
                d_values, d_value_part.reshape(key_len, -1), key_first, 0
            )
            return (d_query, d_keys, d_values)

        return lax.cond(block_index * key_len <= last_row, grad_live_block, keep_state, carried)

    zero_keys = jnp.zeros((seq_len, HEADS * HD), jnp.float32)
    start_grads = (jnp.zeros((row_count, HEADS, HD), jnp.float32), zero_keys, zero_keys)
    d_query, d_keys, d_values = lax.fori_loop(0, key_count, grad_step, start_grads)
    own_keys, own_values = (
        lax.psum_scatter(
            d_keys.astype(jnp.bfloat16), "rep", scatter_dimension=0, tiled=True
        ).astype(jnp.float32),
        lax.psum_scatter(
            d_values.astype(jnp.bfloat16), "rep", scatter_dimension=0, tiled=True
        ).astype(jnp.float32),
    )
    d_projected = jnp.stack(
        [
            rotate_back(
                d_query.reshape(row_count, -1) * score_scale, cosine_table, sine_table, HEADS
            ),
            rotate_back(own_keys, cosine_table, sine_table, HEADS),
            own_values,
        ]
    ).astype(jnp.bfloat16)
    d_qkv = jnp.einsum("ld,jlf->jdf", normed_low, d_projected, preferred_element_type=jnp.float32)
    d_bias = jnp.sum(d_projected.astype(jnp.float32), axis=1)
    d_normed_in = jnp.einsum(
        "jlf,jdf->ld", d_projected, qkv_all, preferred_element_type=jnp.float32
    )
    d_x_norm, d_attn_gain = norm_back(x_rows, attn_gain_float, d_normed_in)
    d_input_rows = d_mid + d_x_norm
    (
        part_attn_gain,
        part_qkv,
        part_bias,
        part_out,
        part_ffn_gain,
        part_shared_gate_up,
        part_shared_down,
        part_shared_gate,
    ) = (
        lax.psum_scatter(
            d_attn_gain.astype(jnp.bfloat16), "shard", scatter_dimension=0, tiled=True
        ).astype(jnp.float32),
        lax.psum_scatter(
            d_qkv.astype(jnp.bfloat16), "shard", scatter_dimension=1, tiled=True
        ).astype(jnp.float32),
        lax.psum_scatter(
            d_bias.astype(jnp.bfloat16), "shard", scatter_dimension=1, tiled=True
        ).astype(jnp.float32),
        lax.psum_scatter(
            d_out_weight.astype(jnp.bfloat16), "shard", scatter_dimension=0, tiled=True
        ).astype(jnp.float32),
        lax.psum_scatter(
            d_ffn_gain.astype(jnp.bfloat16), "shard", scatter_dimension=0, tiled=True
        ).astype(jnp.float32),
        lax.psum_scatter(
            d_shared_gate_up.astype(jnp.bfloat16), "shard", scatter_dimension=1, tiled=True
        ).astype(jnp.float32),
        lax.psum_scatter(
            d_shared_down.astype(jnp.bfloat16), "shard", scatter_dimension=0, tiled=True
        ).astype(jnp.float32),
        lax.psum_scatter(
            d_shared_gate.astype(jnp.bfloat16), "shard", scatter_dimension=0, tiled=True
        ).astype(jnp.float32),
    )
    (
        sum_attn_gain,
        sum_qkv,
        sum_bias,
        sum_out,
        sum_ffn_gain,
        sum_shared_gate_up,
        sum_shared_down,
        sum_shared_gate,
        sum_expert_gate_up,
        sum_expert_down,
    ) = (
        lax.psum_scatter(
            part_attn_gain.astype(jnp.bfloat16), "rep", scatter_dimension=0, tiled=True
        ).astype(jnp.float32),
        lax.psum_scatter(
            part_qkv.astype(jnp.bfloat16), "rep", scatter_dimension=2, tiled=True
        ).astype(jnp.float32),
        lax.psum_scatter(
            part_bias.astype(jnp.bfloat16), "rep", scatter_dimension=1, tiled=True
        ).astype(jnp.float32),
        lax.psum_scatter(
            part_out.astype(jnp.bfloat16), "rep", scatter_dimension=1, tiled=True
        ).astype(jnp.float32),
        lax.psum_scatter(
            part_ffn_gain.astype(jnp.bfloat16), "rep", scatter_dimension=0, tiled=True
        ).astype(jnp.float32),
        lax.psum_scatter(
            part_shared_gate_up.astype(jnp.bfloat16), "rep", scatter_dimension=2, tiled=True
        ).astype(jnp.float32),
        lax.psum_scatter(
            part_shared_down.astype(jnp.bfloat16), "rep", scatter_dimension=1, tiled=True
        ).astype(jnp.float32),
        lax.psum_scatter(
            part_shared_gate.astype(jnp.bfloat16), "rep", scatter_dimension=0, tiled=True
        ).astype(jnp.float32),
        lax.psum_scatter(
            d_expert_gate_up.astype(jnp.bfloat16), "rep", scatter_dimension=2, tiled=True
        ).astype(jnp.float32),
        lax.psum_scatter(
            d_expert_down.astype(jnp.bfloat16), "rep", scatter_dimension=2, tiled=True
        ).astype(jnp.float32),
    )
    grad_attn_gain, grad_bias, grad_ffn_gain, grad_shared_gate = (
        lax.all_gather(sum_attn_gain, "rep", axis=0, tiled=True),
        lax.all_gather(sum_bias, "rep", axis=1, tiled=True),
        lax.all_gather(sum_ffn_gain, "rep", axis=0, tiled=True),
        lax.all_gather(sum_shared_gate, "rep", axis=0, tiled=True),
    )
    return (
        loss_value,
        out_rows.astype(jnp.bfloat16)[None],
        d_input_rows[None],
        grad_attn_gain,
        sum_qkv,
        grad_bias,
        sum_out,
        grad_ffn_gain,
        sum_shared_gate_up,
        sum_shared_down,
        grad_shared_gate,
        sum_expert_gate_up,
        sum_expert_down,
    )


def solution(mesh):
    return jax.shard_map(
        per_device,
        mesh=mesh,
        in_specs=(
            P("shard", "rep", None),
            P("shard", "rep", None),
            P("shard", "rep"),
            P("shard", None, None),
            P("shard", "rep", None),
            P("shard", "rep", None),
            P("shard"),
            P(None, "shard", None),
            P(None, "shard"),
            P("shard", None),
            P("shard"),
            P(None, "shard", None),
            P("shard", None),
            P("shard"),
            P("shard", None, None, None),
            P("shard", None, None),
        ),
        out_specs=(
            P(),
            P("shard", "rep", None),
            P("shard", "rep", None),
            P("shard"),
            P(None, "shard", "rep"),
            P(None, "shard"),
            P("shard", "rep"),
            P("shard"),
            P(None, "shard", "rep"),
            P("shard", "rep"),
            P("shard"),
            P("shard", None, "rep", None),
            P("shard", None, "rep"),
        ),
        check_vma=False,
    )
```

profile of v0, /device:TPU:0, one launch (start us, length us, event | category | flops | bytes accessed | tf_op | source)
XLA Modules:
  0.0 4715.4 jit_solution(13627095037664239442)
XLA Ops:
  37.7 399.8 %all-gather.12.cloned.1.call-done = bf16[3,2048,2048]{2,1,0:T(8,128)(2,1)} async-done(((bf16[3,512,2048]{2,1,0:T(8,128)(2,1)}), bf16[3,2048,2048]{2,1,0:T(8,128)(2,1)}) %all-gather.12.cloned.1.call-update) | async-done | bytes 25165840 | tf_op jit(solution)/shard_map/all_gather | solution.py:148
  479.5 22.1 scatter_fusion
  513.5 23.4 all-gather.22.cloned.1.call-done
  551.4 136.7 %all-gather.16.cloned.1.call-done = bf16[2048,2048]{1,0:T(8,128)(2,1)} async-done(((bf16[512,2048]{1,0:T(8,128)(2,1)}), bf16[2048,2048]{1,0:T(8,128)(2,1)}) %all-gather.16.cloned.1.call-update) | async-done | bytes 8388624 | tf_op jit(solution)/shard_map/all_gather | solution.py:150
  697.7 149.1 %all_to_all.20 = bf16[8,80,2048]{2,1,0:T(8,128)(2,1)S(1)} all-to-all(bf16[8,80,2048]{2,1,0:T(8,128)(2,1)S(1)} %bitcast.380), channel_id=1, replica_groups=mesh['rep'=8,'shard'=4] {'shard'}, dimensions={0} | all-to-all | bytes 5242880 | tf_op jit(solution)/shard_map/all_to_all | solution.py:250
  879.0 157.9 %all-gather.3 = bf16[4,1,512]{2,1,0:T(2,128)(2,1)S(1)} all-gather(bf16[1,1,512]{2,1,0:T(2,128)(2,1)S(1)} %reshape.520), channel_id=1, replica_groups=mesh['rep'=8,'shard'=4] {'shard'}, dimensions={0}, use_global_device_ids=true | all-gather | bytes 5120 | tf_op jit(solution)/shard_map/all_gather | solution.py:225
  1061.6 497.0 %all-gather.18.cloned.1.call-done = bf16[2,2048,5632]{2,1,0:T(8,128)(2,1)} async-done(((bf16[2,512,5632]{2,1,0:T(8,128)(2,1)}), bf16[2,2048,5632]{2,1,0:T(8,128)(2,1)}) %all-gather.18.cloned.1.call-update) | async-done | bytes 46137360 | tf_op jit(solution)/shard_map/all_gather | solution.py:223
  1558.6 23.8 convolution_bitcast_fusion
  1585.9 364.3 %all-gather.20.cloned.1.call-done = bf16[5632,2048]{1,0:T(8,128)(2,1)} async-done(((bf16[1408,2048]{1,0:T(8,128)(2,1)}), bf16[5632,2048]{1,0:T(8,128)(2,1)}) %all-gather.20.cloned.1.call-update) | async-done | bytes 23068688 | tf_op jit(solution)/shard_map/all_gather | solution.py:224
  1962.9 39.0 all-reduce.9
  2018.3 66.2 %scatter_fusion.1 = bf16[8,80,2048]{2,1,0:T(8,128)(2,1)S(1)} fusion(bf16[8,80,2048]{2,1,0:T(8,128)(2,1)S(1)} %broadcast_in_dim.149, s32[512]{0:T(512)S(1)} %bitcast.379, bf16[512,2048]{1,0:T(8,128)(2,1)} %multiply_convert_fusion.1), kind=kCustom, calls=%fused_computation.10 | custom fusion | bytes 6295552 | tf_op jit(solution)/shard_map/scatter | solution.py:290
  2084.4 62.4 %all_to_all.21 = bf16[8,80,2048]{2,1,0:T(8,128)(2,1)} all-to-all(bf16[8,80,2048]{2,1,0:T(8,128)(2,1)S(1)} %scatter_fusion.1), channel_id=1, replica_groups=mesh['rep'=8,'shard'=4] {'shard'}, dimensions={0} | all-to-all | bytes 5242880 | tf_op jit(solution)/shard_map/all_to_all | solution.py:292
  2180.5 15.3 fusion.118
  2195.8 42.5 all-to-all-done.3
  2259.4 23.0 multiply_reduce_fusion.1
  2292.4 27.9 conditional.5
  2338.5 38.8 reduce-scatter.19.cloned.1.call-done
  2387.2 45.8 reduce-scatter.21.cloned.1.call-done
  2469.1 19.9 convert_bitcast_fusion
  2500.5 101.9 %reduce-scatter.27.cloned.1.call-done = bf16[512,2048]{1,0:T(8,128)(2,1)} async-done(((bf16[2048,2048]{1,0:T(8,128)(2,1)}), bf16[512,2048]{1,0:T(8,128)(2,1)}) %reduce-scatter.27.cloned.1.call-update) | async-done | bytes 2097168 | tf_op jit(solution)/shard_map/reduce_scatter | solution.py:403
  2602.5 19.1 fusion.83
  2621.7 364.6 %reduce-scatter.35.cloned.1.call-done = bf16[1408,2048]{1,0:T(8,128)(2,1)} async-done(((bf16[5632,2048]{1,0:T(8,128)(2,1)}), bf16[1408,2048]{1,0:T(8,128)(2,1)}) %reduce-scatter.35.cloned.1.call-update) | async-done | bytes 5767184 | tf_op jit(solution)/shard_map/reduce_scatter | solution.py:412
  2986.3 418.4 %reduce-scatter.23.cloned.1.call-done = bf16[3,512,2048]{1,2,0:T(8,128)(2,1)} async-done(((bf16[3,2048,2048]{1,2,0:T(8,128)(2,1)}), bf16[3,512,2048]{1,2,0:T(8,128)(2,1)}) %reduce-scatter.23.cloned.1.call-update) | async-done | bytes 6291472 | tf_op jit(solution)/shard_map/reduce_scatter | solution.py:397
  3404.8 757.6 %reduce-scatter.31.cloned.1.call-done = bf16[2,512,5632]{1,2,0:T(8,128)(2,1)} async-done(((bf16[2,2048,5632]{1,2,0:T(8,128)(2,1)}), bf16[2,512,5632]{1,2,0:T(8,128)(2,1)}) %reduce-scatter.31.cloned.1.call-update) | async-done | bytes 11534352 | tf_op jit(solution)/shard_map/reduce_scatter | solution.py:409
  4167.7 14.1 fusion.130
  4181.8 19.2 all-reduce.12
  4239.3 51.6 %reduce-scatter.41.cloned.1.call-done = bf16[2,1408,256]{2,1,0:T(8,128)(2,1)} async-done(((bf16[2,1408,2048]{2,1,0:T(8,128)(2,1)}), bf16[2,1408,256]{2,1,0:T(8,128)(2,1)}) %reduce-scatter.41.cloned.1.call-update) | async-done | bytes 1441808 | tf_op jit(solution)/shard_map/reduce_scatter | solution.py:458
  4294.1 41.2 reduce-scatter.29.cloned.1.call-done
  4337.1 148.1 %reduce-scatter.39.cloned.1.call-done = bf16[2,2,256,1408]{2,3,1,0:T(8,128)(2,1)} async-done(((bf16[2,2,2048,1408]{2,3,1,0:T(8,128)(2,1)}), bf16[2,2,256,1408]{2,3,1,0:T(8,128)(2,1)}) %reduce-scatter.39.cloned.1.call-update) | async-done | bytes 2883600 | tf_op jit(solution)/shard_map/reduce_scatter | solution.py:455
  4490.3 57.6 %reduce-scatter.37.cloned.1.call-done = bf16[1408,256]{1,0:T(8,128)(2,1)} async-done(((bf16[1408,2048]{1,0:T(8,128)(2,1)}), bf16[1408,256]{1,0:T(8,128)(2,1)}) %reduce-scatter.37.cloned.1.call-update) | async-done | bytes 720912 | tf_op jit(solution)/shard_map/reduce_scatter | solution.py:449
  4550.2 62.8 %reduce-scatter.25.cloned.1.call-done = bf16[3,512,256]{1,2,0:T(8,128)(2,1)} async-done(((bf16[3,512,2048]{1,2,0:T(8,128)(2,1)}), bf16[3,512,256]{1,2,0:T(8,128)(2,1)}) %reduce-scatter.25.cloned.1.call-update) | async-done | bytes 786448 | tf_op jit(solution)/shard_map/reduce_scatter | solution.py:434
  4615.6 88.0 %reduce-scatter.33.cloned.1.call-done = bf16[2,512,704]{1,2,0:T(8,128)(2,1)} async-done(((bf16[2,512,5632]{1,2,0:T(8,128)(2,1)}), bf16[2,512,704]{1,2,0:T(8,128)(2,1)}) %reduce-scatter.33.cloned.1.call-update) | async-done | bytes 1441808 | tf_op jit(solution)/shard_map/reduce_scatter | solution.py:446
  (364 shorter events, 447.5 us)
Async XLA Ops:
  7.2 430.4 %all-gather.12.cloned.1.call-start = ((), (), s32[]{:S(2)}) async-start(), calls=%async_computation.18 | async-start | bytes 31457280 | tf_op jit(solution)/shard_map/all_gather | solution.py:148
  7.9 493.8 %all-gather.14.cloned.1.call-start = ((), (), s32[]{:S(2)}) async-start(), calls=%async_computation.19 | async-start | bytes 4718592 | tf_op jit(solution)/shard_map/all_gather | solution.py:161
  21.6 426.2 %copy-start.37 = (f32[4,1,512]{2,1,0:T(1,128)}, f32[4,1,512]{2,1,0:T(1,128)S(1)}, u32[]{:S(2)}) copy-start(f32[4,1,512]{2,1,0:T(1,128)S(1)} %convert_element_type.316) | copy-start | bytes 24580
  36.0 420.2 %copy-start.35 = (f32[128,128]{0,1:T(8,128)}, f32[128,128]{0,1:T(8,128)S(1)}, u32[]{:S(2)}) copy-start(f32[128,128]{0,1:T(8,128)S(1)} %copy.184) | copy-start | bytes 196612
  37.7 410.1 %copy-start.44 = (f32[128]{0:T(128)}, f32[128]{0:T(128)S(1)}, u32[]{:S(2)}) copy-start(f32[128]{0:T(128)S(1)} %add_rsqrt_fusion.1) | copy-start | bytes 1540
  462.7 74.3 %all-gather.22.cloned.1.call-start = ((), (), s32[]{:S(2)}) async-start(), calls=%async_computation.35 | async-start | bytes 4718592 | tf_op jit(solution)/shard_map/all_gather | solution.py:162
  463.6 224.4 %all-gather.16.cloned.1.call-start = ((), (), s32[]{:S(2)}) async-start(), calls=%async_computation.20 | async-start | bytes 10485760 | tf_op jit(solution)/shard_map/all_gather | solution.py:150
  464.2 1094.4 %all-gather.18.cloned.1.call-start = ((), (), s32[]{:S(2)}) async-start(), calls=%async_computation.21 | async-start | bytes 57671680 | tf_op jit(solution)/shard_map/all_gather | solution.py:223
  464.8 1485.4 %all-gather.20.cloned.1.call-start = ((), (), s32[]{:S(2)}) async-start(), calls=%async_computation.22 | async-start | bytes 28835840 | tf_op jit(solution)/shard_map/all_gather | solution.py:224
  538.0 150.0 %copy-start.13 = (bf16[1,128,2048]{2,1,0:T(8,128)(2,1)S(1)}, bf16[1,128,2048]{2,1,0:T(8,128)(2,1)}, u32[]{:S(2)}) copy-start(bf16[1,128,2048]{2,1,0:T(8,128)(2,1)} %param.26) | copy-start | bytes 1572868
  551.1 141.7 %copy-start.18 = (f32[128,16,128]{2,0,1:T(8,128)}, f32[128,16,128]{2,0,1:T(8,128)S(1)}, u32[]{:S(2)}) copy-start(f32[128,16,128]{2,0,1:T(8,128)S(1)} %get-tuple-element.489) | copy-start | bytes 3145732
  551.4 141.4 %copy-start.15 = (bf16[128,16,128]{0,2,1:T(8,128)(2,1)}, bf16[128,16,128]{0,2,1:T(8,128)(2,1)S(1)}, u32[]{:S(2)}) copy-start(bf16[128,16,128]{0,2,1:T(8,128)(2,1)S(1)} %copy.191) | copy-start | bytes 1572868
  694.0 864.6 %copy-start.2 = (bf16[128,2048]{1,0:T(8,128)(2,1)}, bf16[128,2048]{1,0:T(8,128)(2,1)S(1)}, u32[]{:S(2)}) copy-start(bf16[128,2048]{1,0:T(8,128)(2,1)S(1)} %multiply_convert_fusion.7) | copy-start | bytes 1572868
  872.7 164.2 %copy-start.61 = (s32[1,128]{1,0:T(1,128)S(1)}, s32[1,128]{1,0:T(1,128)}, u32[]{:S(2)}) copy-start(s32[1,128]{1,0:T(1,128)} %param.28) | copy-start | bytes 1540
  874.5 164.3 %all-to-all-start.1 = ((bf16[8,80,2048]{2,1,0:T(8,128)(2,1)}), bf16[8,80,2048]{2,1,0:T(8,128)(2,1)S(1)}, u32[]{:S(2)}, u32[]{:S(2)}) async-start(bf16[8,80,2048]{2,1,0:T(8,128)(2,1)} %bitcast.382), calls=%async_computation.1 | async-start | bytes 5242880 | tf_op jit(solution)/shard_map/all_to_all | solution.py:255
  1585.9 373.7 %copy-start.7 = (bf16[128,5632]{1,0:T(8,128)(2,1)}, bf16[128,5632]{1,0:T(8,128)(2,1)S(1)}, u32[]{:S(2)}) copy-start(bf16[128,5632]{1,0:T(8,128)(2,1)S(1)} %multiply_convert_fusion.5) | copy-start | bytes 4325380
  1585.9 373.7 %copy-start.5 = (f32[128,2048]{1,0:T(8,128)S(1)}, f32[128,2048]{1,0:T(8,128)}, u32[]{:S(2)}) copy-start(f32[128,2048]{1,0:T(8,128)} %copy-done.4) | copy-start | bytes 3145732
  2176.1 62.1 %all-to-all-start.3 = ((bf16[8,80,2048]{2,1,0:T(8,128)(2,1)}), bf16[8,80,2048]{2,1,0:T(8,128)(2,1)S(1)}, u32[]{:S(2)}, u32[]{:S(2)}) async-start(bf16[8,80,2048]{2,1,0:T(8,128)(2,1)} %bitcast.381), calls=%async_computation.3 | async-start | bytes 5242880 | tf_op jit(solution)/shard_map/all_to_all | solution.py:299
  2179.8 197.5 %reduce-scatter.19.cloned.1.call-start = ((), (), s32[]{:S(2)}) async-start(), calls=%async_computation.23 | async-start | bytes 4718592 | tf_op jit(solution)/shard_map/reduce_scatter | solution.py:361
  2326.9 106.1 %reduce-scatter.21.cloned.1.call-start = ((), (), s32[]{:S(2)}) async-start(), calls=%async_computation.24 | async-start | bytes 4718592 | tf_op jit(solution)/shard_map/reduce_scatter | solution.py:364
  2333.6 155.5 %reduce-scatter.43.cloned.1.call-start = ((), (), s32[]{:S(2)}) async-start(), calls=%async_computation.36 | async-start | bytes 655360
  2435.6 166.8 %reduce-scatter.27.cloned.1.call-start = ((), (), s32[]{:S(2)}) async-start(), calls=%async_computation.27 | async-start | bytes 10485760 | tf_op jit(solution)/shard_map/reduce_scatter | solution.py:403
  2441.2 545.0 %reduce-scatter.35.cloned.1.call-start = ((), (), s32[]{:S(2)}) async-start(), calls=%async_computation.31 | async-start | bytes 28835840 | tf_op jit(solution)/shard_map/reduce_scatter | solution.py:412
  2453.6 951.1 %reduce-scatter.23.cloned.1.call-start = ((), (), s32[]{:S(2)}) async-start(), calls=%async_computation.25 | async-start | bytes 31457280 | tf_op jit(solution)/shard_map/reduce_scatter | solution.py:397
  2467.6 1694.8 %reduce-scatter.31.cloned.1.call-start = ((), (), s32[]{:S(2)}) async-start(), calls=%async_computation.29 | async-start | bytes 57671680 | tf_op jit(solution)/shard_map/reduce_scatter | solution.py:409
  2489.0 1739.9 %reduce-scatter.45.cloned.1.call-start = ((), (), s32[]{:S(2)}) async-start(), calls=%async_computation.37 | async-start | bytes 147456
  2489.6 1801.3 %reduce-scatter.41.cloned.1.call-start = ((), (), s32[]{:S(2)}) async-start(), calls=%async_computation.34 | async-start | bytes 12976128 | tf_op jit(solution)/shard_map/reduce_scatter | solution.py:458
  2500.5 1834.8 %reduce-scatter.29.cloned.1.call-start = ((), (), s32[]{:S(2)}) async-start(), calls=%async_computation.28 | async-start | bytes 2359296 | tf_op jit(solution)/shard_map/reduce_scatter | solution.py:440
  2602.5 1882.7 %reduce-scatter.39.cloned.1.call-start = ((), (), s32[]{:S(2)}) async-start(), calls=%async_computation.33 | async-start | bytes 25952256 | tf_op jit(solution)/shard_map/reduce_scatter | solution.py:455
  2621.6 1926.3 %reduce-scatter.37.cloned.1.call-start = ((), (), s32[]{:S(2)}) async-start(), calls=%async_computation.32 | async-start | bytes 6488064 | tf_op jit(solution)/shard_map/reduce_scatter | solution.py:449
  2986.2 1626.8 %reduce-scatter.25.cloned.1.call-start = ((), (), s32[]{:S(2)}) async-start(), calls=%async_computation.26 | async-start | bytes 7077888 | tf_op jit(solution)/shard_map/reduce_scatter | solution.py:434
  3404.8 1298.8 %reduce-scatter.33.cloned.1.call-start = ((), (), s32[]{:S(2)}) async-start(), calls=%async_computation.30 | async-start | bytes 12976128 | tf_op jit(solution)/shard_map/reduce_scatter | solution.py:446
  (54 other events, 526.1 us)
Sparse Core Ops, SparseCore 0:
  9.6 427.9 all-gather.11
  462.8 34.8 all-gather.13
  500.2 36.7 all-gather.21
  538.4 149.6 all-gather.15
  689.5 869.0 all-gather.17
  1560.1 390.1 all-gather.19
  2327.0 50.2 reduce-scatter.18
  2381.6 51.2 reduce-scatter.20
  2435.8 21.6 reduce-scatter.42
  2459.7 142.7 reduce-scatter.26
  2604.8 381.3 reduce-scatter.34
  2988.6 416.1 reduce-scatter.22
  3407.1 755.2 reduce-scatter.30
  4165.6 35.1 reduce-scatter.44
  4204.1 86.8 reduce-scatter.40
  4294.0 41.2 reduce-scatter.28
  4339.2 145.9 reduce-scatter.38
  4488.8 59.0 reduce-scatter.36
  4551.3 61.7 reduce-scatter.24
  4616.8 86.7 reduce-scatter.32
where the time goes:
time: 4720 us
  waiting for transfers between devices  3640 us (77%)
  blocking collectives  500 us (11%)
  matrix products  271 us (6%)
  local copies, waits for them, and re-layouts  206 us (4%)
  other arithmetic  65.4 us (1%)
    reduce_scatter x1, waiting for transfers between devices, per_device(): lax.psum_scatter(d_shared_gate_up.astype(jnp.bfloat16), 'shard', scatter_...  758 us
    all_gather x1, waiting for transfers between devices, per_device(): lax.all_gather(shared_gate_up, 'shard', axis=1, tiled=True)  497 us
    reduce_scatter x1, waiting for transfers between devices, per_device(): lax.psum_scatter(d_qkv.astype(jnp.bfloat16), 'shard', scatter_dimension=1...  418 us
    all_gather x1, waiting for transfers between devices, per_device(): lax.all_gather(w_qkv, 'shard', axis=1, tiled=True)  400 us
    reduce_scatter x1, waiting for transfers between devices, per_device(): lax.psum_scatter(d_shared_down.astype(jnp.bfloat16), 'shard', scatter_dim...  365 us
    all_gather x1, waiting for transfers between devices, per_device(): lax.all_gather(shared_down, 'shard', axis=0, tiled=True)  364 us
    all_gather x1, blocking collectives, per_device(): lax.all_gather(shared_gate, 'shard', axis=0, tiled=True)  158 us
    all_to_all x1, blocking collectives, per_device(): lax.all_to_all(token_buffer, 'shard', split_axis=0, concat_axis=0, tiled=...  149 us
  transfers between devices with their start and end apart: 22, of which 18 were waited for; matrix products, arithmetic and copies ran while one was open for 6% of the time, Pallas kernels for 0%

commit v1 on v0

--- a/solution.py
+++ b/solution.py
@@ -482,9 +482,376 @@
     )
 
 
+def flip_pairs(count, bit):
+    return [(place, place ^ bit) for place in range(count)]
+
+
+def exchange(values, replicas, bit):
+    return lax.ppermute(values, "rep", flip_pairs(replicas, bit))
+
+
+def take_one(values, place, axis):
+    return lax.dynamic_index_in_dim(values, place, axis, keepdims=False)
+
+
+def add_low(first, second):
+    return (first.astype(jnp.float32) + second.astype(jnp.float32)).astype(jnp.bfloat16)
+
+
+def sum_over_chips(values, replicas, axis, row_first):
+    place = lax.axis_index("rep")
+    bits = (2, 4) if row_first else (4, 2)
+    shape = values.shape
+    values = values.reshape(shape[:axis] + (2, 2) + shape[axis + 1 :])
+    if not row_first:
+        values = jnp.swapaxes(values, axis, axis + 1)
+    for bit, at in zip(bits, (axis + 1, axis)):
+        mine = (place // bit) % 2
+        kept = take_one(values, mine, at)
+        values = add_low(kept, exchange(take_one(values, 1 - mine, at), replicas, bit))
+    return values
+
+
+def per_device_heads(
+    tokens,
+    teacher,
+    valid_mask,
+    block_mask,
+    routes,
+    gates,
+    attn_gain,
+    w_qkv,
+    qkv_bias,
+    w_out,
+    ffn_gain,
+    shared_gate_up,
+    shared_down,
+    shared_gate,
+    expert_gate_up,
+    expert_down,
+):
+    x_rows = tokens[0].astype(jnp.float32)
+    row_count, model_width = x_rows.shape
+    groups = lax.axis_size("shard")
+    replicas = lax.axis_size("rep")
+    halves = replicas // groups
+    place = lax.axis_index("rep")
+    group = lax.axis_index("shard")
+    core = place % 2
+    seq_len = row_count * replicas
+    heads = HEADS // replicas
+    head_cols = heads * HD
+    slice_rows = w_qkv.shape[1]
+    hidden_all = shared_gate_up.shape[2]
+    hidden_cols = hidden_all // replicas
+    out_cols = model_width // replicas
+    score_scale = 1.0 / math.sqrt(HD)
+
+    valid_rows = valid_mask[0].astype(jnp.float32)
+    count_total = lax.psum(jnp.sum(valid_rows), ("rep", "shard"))
+
+    vectors = jnp.concatenate(
+        [attn_gain[None], ffn_gain[None], shared_gate[None], qkv_bias], axis=0
+    )
+    vectors = lax.all_gather(vectors, "shard", axis=1, tiled=True).astype(jnp.float32)
+    attn_gain_float, ffn_gain_float, shared_gate_float = vectors[0], vectors[1], vectors[2]
+    bias_float = lax.dynamic_slice_in_dim(vectors[3:], place * head_cols, head_cols, 1)
+
+    qkv_weight = lax.all_gather(
+        lax.dynamic_slice_in_dim(w_qkv, place * head_cols, head_cols, 2),
+        "shard",
+        axis=1,
+        tiled=True,
+    )
+    normed_low = (x_rows * norm_scale(x_rows) * attn_gain_float).astype(jnp.bfloat16)
+    normed_seq = lax.all_gather(normed_low, "rep", axis=0, tiled=True)
+
+    down_part = shared_down.reshape(halves, replicas, -1, model_width)
+    out_part = w_out.reshape(halves, replicas, -1, model_width)
+    down_rows = down_part.shape[2]
+    row_part = jnp.concatenate([take_one(down_part, place, 1), take_one(out_part, place, 1)], axis=1)
+    row_part = lax.all_gather(row_part, "shard", axis=0, tiled=True)
+    row_part = lax.all_to_all(row_part, "rep", split_axis=0, concat_axis=0, tiled=True)
+    down_weight = row_part[:, :down_rows].reshape(-1, model_width)
+    out_weight = row_part[:, down_rows:].reshape(-1, model_width)
+
+    gate_up_weight = lax.all_gather(
+        lax.dynamic_slice_in_dim(shared_gate_up, place * hidden_cols, hidden_cols, 2),
+        "shard",
+        axis=1,
+        tiled=True,
+    )
+
+    projected = jnp.einsum(
+        "ld,jdf->jlf", normed_seq, qkv_weight, preferred_element_type=jnp.float32
+    )
+    projected = projected + bias_float[:, None, :]
+    cosine_table, sine_table = rope_tables(0, seq_len, HD)
+    query_low = rotate(projected[0], cosine_table, sine_table, heads).astype(jnp.bfloat16)
+    key_low = rotate(projected[1], cosine_table, sine_table, heads).astype(jnp.bfloat16)
+    value_low = projected[2].astype(jnp.bfloat16)
+    query_heads = query_low.reshape(seq_len, heads, HD)
+    key_heads = key_low.reshape(seq_len, heads, HD)
+    value_heads = value_low.reshape(seq_len, heads, HD)
+    permitted = allowed_keys(block_mask[0], 0, seq_len, 0, seq_len, BLOCK)[None]
+    scores = (
+        jnp.einsum("qhd,khd->hqk", query_heads, key_heads, preferred_element_type=jnp.float32)
+        * score_scale
+    )
+    scores = jnp.where(permitted, scores, NEG)
+    terms = jnp.exp(scores - jnp.max(scores, axis=-1, keepdims=True))
+    probs = terms / jnp.sum(terms, axis=-1, keepdims=True)
+    probs_low = probs.astype(jnp.bfloat16)
+    attended = jnp.einsum(
+        "hqk,khd->qhd", probs_low, value_heads, preferred_element_type=jnp.float32
+    )
+    attended_low = attended.reshape(seq_len, head_cols).astype(jnp.bfloat16)
+    branch = jnp.dot(attended_low, out_weight, preferred_element_type=jnp.float32)
+    mid_rows = x_rows + lax.psum_scatter(
+        branch.astype(jnp.bfloat16), "rep", scatter_dimension=0, tiled=True
+    ).astype(jnp.float32)
+    normed_mid = (mid_rows * norm_scale(mid_rows) * ffn_gain_float).astype(jnp.bfloat16)
+
+    def gather_column(values):
+        own = lax.all_gather(values, "shard", axis=0, tiled=False)
+        return jnp.concatenate([own, exchange(own, replicas, 1)], axis=0)
+
+    def scatter_column(parts):
+        own = add_low(parts[:groups], exchange(parts[groups:], replicas, 1))
+        return lax.psum_scatter(own, "shard", scatter_dimension=0, tiled=False)
+
+    experts_total = groups * expert_gate_up.shape[0]
+    route_weight = jnp.sum(
+        jnp.where(
+            routes[0][:, :, None] == jnp.arange(experts_total, dtype=jnp.int32),
+            gates[0][:, :, None],
+            0.0,
+        ),
+        axis=1,
+    )
+    column_weight = gather_column(route_weight)
+    mine = group * 2 + core
+    my_weight = take_one(column_weight, mine, 2)
+    chosen = my_weight > 0
+    slot = jnp.cumsum(chosen.astype(jnp.int32), axis=1) - 1
+    pick = chosen[:, None, :] & (
+        slot[:, None, :] == jnp.arange(CAP, dtype=jnp.int32)[None, :, None]
+    )
+    slot_weight = jnp.sum(jnp.where(pick, my_weight[:, None, :], 0.0), axis=2)
+    pick_low = pick.astype(jnp.bfloat16)
+    my_gate_up = take_one(expert_gate_up, core, 0)
+    my_down = take_one(expert_down, core, 0)
+
+    def to_slots(values):
+        return jnp.einsum(
+            "bst,btd->bsd", pick_low, values, preferred_element_type=jnp.float32
+        ).astype(jnp.bfloat16)
+
+    def from_slots(values):
+        return jnp.einsum(
+            "bst,bsd->btd", pick_low, values, preferred_element_type=jnp.float32
+        ).astype(jnp.bfloat16)
+
+    mid_column = gather_column(normed_mid)
+    mid_seq = lax.all_gather(normed_mid, "rep", axis=0, tiled=True)
+
+    expert_in = to_slots(mid_column).reshape(-1, model_width)
+    expert_pre = jnp.einsum(
+        "sd,jdf->jsf", expert_in, my_gate_up, preferred_element_type=jnp.float32
+    )
+    expert_hidden = swiglu(expert_pre[0], expert_pre[1]).astype(jnp.bfloat16)
+    expert_out = jnp.dot(expert_hidden, my_down, preferred_element_type=jnp.float32)
+    expert_out = expert_out.reshape(slot_weight.shape + (model_width,))
+    expert_out = (slot_weight[:, :, None] * expert_out).astype(jnp.bfloat16)
+    expert_mix = scatter_column(from_slots(expert_out))
+
+    shared_pre = jnp.einsum(
+        "ld,jdf->jlf", mid_seq, gate_up_weight, preferred_element_type=jnp.float32
+    )
+    shared_hidden = swiglu(shared_pre[0], shared_pre[1]).astype(jnp.bfloat16)
+    shared_weight = jax.nn.sigmoid(
+        jnp.sum(mid_seq.astype(jnp.float32) * shared_gate_float[None, :], axis=1)
+    )
+    shared_out = jnp.dot(shared_hidden, down_weight, preferred_element_type=jnp.float32)
+    shared_mix = lax.psum_scatter(
+        (shared_weight[:, None] * shared_out).astype(jnp.bfloat16),
+        "rep",
+        scatter_dimension=0,
+        tiled=True,
+    )
+
+    out_rows = mid_rows + (shared_mix.astype(jnp.float32) + expert_mix.astype(jnp.float32))
+    diff_rows = out_rows - teacher[0].astype(jnp.float32)
+    squares_local = jnp.sum(valid_rows * jnp.sum(diff_rows * diff_rows, axis=1))
+    tokens_all = row_count * replicas * groups
+    d_rows = valid_rows[:, None] * diff_rows * (tokens_all / (2.0 * count_total))
+    d_low = d_rows.astype(jnp.bfloat16)
+    d_column = gather_column(d_low)
+    d_seq = lax.all_gather(d_low, "rep", axis=0, tiled=True)
+
+    d_expert_out = (slot_weight[:, :, None] * to_slots(d_column).astype(jnp.float32)).astype(
+        jnp.bfloat16
+    )
+    d_expert_out = d_expert_out.reshape(-1, model_width)
+    d_expert_hidden = jnp.einsum(
+        "sd,fd->sf", d_expert_out, my_down, preferred_element_type=jnp.float32
+    )
+    d_gate_expert, d_up_expert = swiglu_grads(expert_pre[0], expert_pre[1], d_expert_hidden)
+    d_expert_pre = jnp.stack([d_gate_expert, d_up_expert]).astype(jnp.bfloat16)
+    d_expert_in = jnp.einsum(
+        "jsf,jdf->sd", d_expert_pre, my_gate_up, preferred_element_type=jnp.float32
+    ).astype(jnp.bfloat16)
+    d_expert_in = d_expert_in.reshape(slot_weight.shape + (model_width,))
+    d_mid_experts = scatter_column(from_slots(d_expert_in))
+
+    d_shared_out = (shared_weight[:, None] * d_seq.astype(jnp.float32)).astype(jnp.bfloat16)
+    d_plain_hidden = jnp.einsum(
+        "ld,fd->lf", d_seq, down_weight, preferred_element_type=jnp.float32
+    )
+    d_logit = (
+        jnp.sum(shared_hidden.astype(jnp.float32) * d_plain_hidden, axis=1)
+        * shared_weight
+        * (1.0 - shared_weight)
+    )
+    d_gate_shared, d_up_shared = swiglu_grads(
+        shared_pre[0], shared_pre[1], shared_weight[:, None] * d_plain_hidden
+    )
+    d_shared_pre = jnp.stack([d_gate_shared, d_up_shared]).astype(jnp.bfloat16)
+    d_mid_shared = jnp.einsum(
+        "jlf,jdf->ld", d_shared_pre, gate_up_weight, preferred_element_type=jnp.float32
+    )
+    d_mid_shared = d_mid_shared + d_logit[:, None] * shared_gate_float[None, :]
+    d_mid_shared = lax.psum_scatter(
+        d_mid_shared.astype(jnp.bfloat16), "rep", scatter_dimension=0, tiled=True
+    )
+
+    d_gate_up_expert = jnp.einsum(
+        "sd,jsf->jdf", expert_in, d_expert_pre, preferred_element_type=jnp.float32
+    ).astype(jnp.bfloat16)
+    d_down_expert = jnp.einsum(
+        "sf,sd->fd", expert_hidden, d_expert_out, preferred_element_type=jnp.float32
+    ).astype(jnp.bfloat16)
+    d_shared_gate_up = jnp.einsum(
+        "ld,jlf->jdf", mid_seq, d_shared_pre, preferred_element_type=jnp.float32
+    ).astype(jnp.bfloat16)
+    d_shared_down = jnp.einsum(
+        "lf,ld->fd", shared_hidden, d_shared_out, preferred_element_type=jnp.float32
+    ).astype(jnp.bfloat16)
+    d_shared_gate = jnp.einsum("l,ld->d", d_logit, mid_seq.astype(jnp.float32))
+
+    chips = replicas // 2
+    expert_width = my_down.shape[0]
+    cut = expert_width // 2
+    grad_parts = (
+        (d_gate_up_expert[0].reshape(chips, -1, expert_width), 0, True),
+        (d_gate_up_expert[1].reshape(chips, -1, expert_width), 0, False),
+        (d_down_expert[:cut].reshape(cut, chips, -1), 1, True),
+        (d_down_expert[cut:].reshape(cut, chips, -1), 1, False),
+    )
+    grad_sums = [sum_over_chips(part, replicas, axis, first) for part, axis, first in grad_parts]
+
+    def split_cores(values, axis):
+        shape = values.shape
+        values = values.reshape(shape[:axis] + (2, -1) + shape[axis + 1 :])
+        kept = take_one(values, core, axis)
+        other = exchange(take_one(values, 1 - core, axis), replicas, 1)
+        low = jnp.where(core == 0, kept, other)
+        high = jnp.where(core == 0, other, kept)
+        return jnp.stack([low, high])
+
+    grad_expert_gate_up = split_cores(jnp.stack(grad_sums[:2]), 1).astype(jnp.float32)
+    grad_expert_down = split_cores(jnp.concatenate(grad_sums[2:], axis=0), 1).astype(jnp.float32)
+
+    grad_shared_gate_up = lax.psum_scatter(
+        d_shared_gate_up, "shard", scatter_dimension=1, tiled=True
+    ).astype(jnp.float32)
+
+    def row_grads(values):
+        spread = lax.all_to_all(values, "rep", split_axis=1, concat_axis=0, tiled=True)
+        return lax.psum_scatter(spread, "shard", scatter_dimension=0, tiled=True).astype(
+            jnp.float32
+        )
+
+    grad_shared_down = row_grads(d_shared_down)
+
+    d_normed_mid = d_mid_shared.astype(jnp.float32) + d_mid_experts.astype(jnp.float32)
+    d_mid_norm, d_ffn_gain = norm_back(mid_rows, ffn_gain_float, d_normed_mid)
+    d_mid = d_rows + d_mid_norm
+    d_branch = lax.all_gather(d_mid.astype(jnp.bfloat16), "rep", axis=0, tiled=True)
+    d_attended = jnp.einsum(
+        "ld,fd->lf", d_branch, out_weight, preferred_element_type=jnp.float32
+    )
+    d_attended = d_attended.astype(jnp.bfloat16).reshape(seq_len, heads, HD)
+    d_out_weight = jnp.einsum(
+        "lf,ld->fd", attended_low, d_branch, preferred_element_type=jnp.float32
+    ).astype(jnp.bfloat16)
+    grad_out = row_grads(d_out_weight)
+
+    d_values = jnp.einsum(
+        "hqk,qhd->khd", probs_low, d_attended, preferred_element_type=jnp.float32
+    )
+    d_probs = jnp.einsum(
+        "qhd,khd->hqk", d_attended, value_heads, preferred_element_type=jnp.float32
+    )
+    delta = jnp.sum(probs * d_probs, axis=-1, keepdims=True)
+    d_scores = (probs * (d_probs - delta)).astype(jnp.bfloat16)
+    d_query = jnp.einsum("hqk,khd->qhd", d_scores, key_heads, preferred_element_type=jnp.float32)
+    d_keys = jnp.einsum("hqk,qhd->khd", d_scores, query_heads, preferred_element_type=jnp.float32)
+    d_projected = jnp.stack(
+        [
+            rotate_back(
+                d_query.reshape(seq_len, -1) * score_scale, cosine_table, sine_table, heads
+            ),
+            rotate_back(d_keys.reshape(seq_len, -1) * score_scale, cosine_table, sine_table, heads),
+            d_values.reshape(seq_len, -1),
+        ]
+    ).astype(jnp.bfloat16)
+    d_qkv = jnp.einsum(
+        "ld,jlf->jdf", normed_seq, d_projected, preferred_element_type=jnp.float32
+    ).astype(jnp.bfloat16)
+    d_bias = jnp.sum(d_projected.astype(jnp.float32), axis=1)
+    grad_qkv = lax.psum_scatter(d_qkv, "shard", scatter_dimension=1, tiled=True).astype(
+        jnp.float32
+    )
+    d_normed_in = jnp.einsum(
+        "jlf,jdf->ld", d_projected, qkv_weight, preferred_element_type=jnp.float32
+    )
+    d_normed_in = lax.psum_scatter(
+        d_normed_in.astype(jnp.bfloat16), "rep", scatter_dimension=0, tiled=True
+    ).astype(jnp.float32)
+    d_x_norm, d_attn_gain = norm_back(x_rows, attn_gain_float, d_normed_in)
+    d_input_rows = d_mid + d_x_norm
+
+    d_bias_all = lax.dynamic_update_slice_in_dim(
+        jnp.zeros((3, model_width), jnp.float32), d_bias, place * head_cols, 1
+    )
+    small = jnp.concatenate(
+        [d_attn_gain[None], d_ffn_gain[None], d_shared_gate[None], d_bias_all], axis=0
+    )
+    small, squares_total = lax.psum((small, squares_local), ("rep", "shard"))
+    small = lax.dynamic_slice_in_dim(small, group * slice_rows, slice_rows, 1)
+    loss_value = squares_total / (count_total * model_width)
+    return (
+        loss_value,
+        out_rows.astype(jnp.bfloat16)[None],
+        d_input_rows[None],
+        small[0],
+        grad_qkv,
+        small[3:],
+        grad_out,
+        small[1],
+        grad_shared_gate_up,
+        grad_shared_down,
+        small[2],
+        grad_expert_gate_up,
+        grad_expert_down,
+    )
+
+
 def solution(mesh):
+    by_heads = mesh.shape["rep"] == 8 and mesh.shape["shard"] == 4
     return jax.shard_map(
-        per_device,
+        per_device_heads if by_heads else per_device,
         mesh=mesh,
         in_specs=(
             P("shard", "rep", None),

time: 4720 us -> 1230 us (0.26)
  waiting for transfers between devices: 3640 us -> 571 us
  blocking collectives: 500 us -> 162 us
  matrix products: 271 us -> 182 us
    reduce_scatter x12 -> x10, waiting for transfers between devices: 2180 us -> 169 us  [the longest x1 54.6 us: per_device_heads(): lax.psum_scatter(d_mid_shared.astype(jnp.bfloat16), 'rep', scatter_dimens...]
    all_gather x6 -> x9, waiting for transfers between devices: 1420 us -> 317 us  [the longest x2 87.6 us: gather_column(): own = lax.all_gather(values, 'shard', axis=0, tiled=False)]
    all_gather x5 -> x2, blocking collectives: 206 us -> 28.2 us  [the longest x1 14.8 us: per_device_heads(): lax.all_gather(vectors, 'shard', axis=1, tiled=True).astype(jnp.float32)]
    all_to_all x2 -> x1, blocking collectives: 211 us -> 53 us  [row_grads(): lax.all_to_all(values, 'rep', split_axis=1, concat_axis=0, tiled=True)]
    dot_general x27, matrix products: 271 us -> 173 us  [the longest x1 13.8 us: per_device_heads(): jnp.einsum('sd,jsf->jdf', expert_in, d_expert_pre, preferred_element_type...]
    scatter x2 -> x0, local copies, waits for them, and re-layouts: 88.3 us -> none  [the longest x1 66.2 us: per_device(): d_buffer = jnp.zeros((experts_total, CAP, model_width), jnp.bfloat16).at[...]
    ppermute x0 -> x15, waiting for transfers between devices: none -> 72.1 us  [exchange(): return lax.ppermute(values, 'rep', flip_pairs(replicas, bit))]
    another operation x9 -> x11, local copies, waits for them, and re-layouts: 8.29 us -> 58.8 us  [the longest x4 36.5 us: sum_over_chips(): values = values.reshape(shape[:axis] + (2, 2) + shape[axis + 1:])]
  transfers between devices with their start and end apart: 22 -> 36, of which waited for: 18 -> 19; matrix products, arithmetic and copies ran while one was open for 6% -> 34% of each run, Pallas kernels for 0% -> 0%
where the time goes in v1:
time: 1230 us; the launch traced here: 1220 us
  waiting for transfers between devices  571 us (46%)
  local copies, waits for them, and re-layouts  191 us (16%)
  matrix products  182 us (15%)
  blocking collectives  162 us (13%)
  other arithmetic  76.5 us (6%)
  starting transfers between devices  21.5 us (2%)
  between operations  18.5 us (2%)
    all_gather x2, waiting for transfers between devices, gather_column(): own = lax.all_gather(values, 'shard', axis=0, tiled=False)  87.6 us
    all_gather x1, waiting for transfers between devices, per_device_heads(): lax.all_gather(lax.dynamic_slice_in_dim(shared_gate_up, place * hidden_co...  86.8 us
    ppermute x15, waiting for transfers between devices, exchange(): return lax.ppermute(values, 'rep', flip_pairs(replicas, bit))  72.1 us
    all_gather x1, waiting for transfers between devices, per_device_heads(): lax.all_gather(lax.dynamic_slice_in_dim(w_qkv, place * head_cols, head_co...  59.3 us
    unnamed x143, local copies, waits for them, and re-layouts  57.5 us
    reduce_scatter x1, waiting for transfers between devices, per_device_heads(): lax.psum_scatter(d_mid_shared.astype(jnp.bfloat16), 'rep', scatter_dimens...  54.6 us
    all_to_all x1, blocking collectives, row_grads(): lax.all_to_all(values, 'rep', split_axis=1, concat_axis=0, tiled=True)  53 us
    reduce_scatter x1, waiting for transfers between devices, per_device_heads(): lax.psum_scatter(branch.astype(jnp.bfloat16), 'rep', scatter_dimension=0,...  51.5 us
  transfers between devices with their start and end apart: 36, of which 19 were waited for; matrix products, arithmetic and copies ran while one was open for 34% of the time, Pallas kernels for 0%

profile of v1, /device:TPU:0, one launch (start us, length us, event | category | flops | bytes accessed | tf_op | source)
XLA Modules:
  0.0 1221.6 jit_solution(6140246711698672143)
XLA Ops:
  13.8 14.8 %all_gather.43 = bf16[6,2048]{1,0:T(8,128)(2,1)S(1)} all-gather(bf16[6,512]{1,0:T(8,128)(2,1)S(1)} %pad_maximum_fusion.11), channel_id=1, replica_groups=mesh['rep'=8,'shard'=4] {'shard'}, dimensions={1}, use_global_device_ids=true | all-gather | bytes 30720 | tf_op jit(solution)/shard_map/all_gather | solution.py:556
  45.0 45.5 %all-gather.17.cloned.1.call-done = bf16[8,120,2048]{2,1,0:T(8,128)(2,1)} async-done(((bf16[2,120,2048]{2,1,0:T(8,128)(2,1)}), bf16[8,120,2048]{2,1,0:T(8,128)(2,1)}) %all-gather.17.cloned.1.call-update) | async-done | bytes 3932176 | tf_op jit(solution)/shard_map/all_gather | solution.py:573
  95.4 59.3 %all-gather.13.cloned.1.call-done = bf16[3,2048,256]{1,2,0:T(8,128)(2,1)} async-done(((bf16[3,512,256]{1,2,0:T(8,128)(2,1)}), bf16[3,2048,256]{1,2,0:T(8,128)(2,1)}) %all-gather.13.cloned.1.call-update) | async-done | bytes 3145744 | tf_op jit(solution)/shard_map/all_gather | solution.py:560
  154.6 37.9 %all-gather.15.cloned.1.call-done = bf16[1024,2048]{1,0:T(8,128)(2,1)} async-done(((bf16[128,2048]{1,0:T(8,128)(2,1)}), bf16[1024,2048]{1,0:T(8,128)(2,1)}) %all-gather.15.cloned.1.call-update) | async-done | bytes 4194320 | tf_op jit(solution)/shard_map/all_gather | solution.py:567
  218.9 51.5 %reduce-scatter.11.cloned.1.call-done = bf16[128,2048]{1,0:T(8,128)(2,1)} async-done(((bf16[1024,2048]{1,0:T(8,128)(2,1)}), bf16[128,2048]{1,0:T(8,128)(2,1)}) %reduce-scatter.11.cloned.1.call-update) | async-done | bytes 524304 | tf_op jit(solution)/shard_map/reduce_scatter | solution.py:610
  278.2 41.6 %all-gather.27.cloned.1.call-done = bf16[512,2048]{1,0:T(8,128)(2,1)} async-done(((bf16[128,2048]{1,0:T(8,128)(2,1)}), bf16[512,2048]{1,0:T(8,128)(2,1)}) %all-gather.27.cloned.1.call-update) | async-done | bytes 2097168 | tf_op jit(solution)/shard_map/all_gather | solution.py:616
  319.8 13.4 %all-gather = f32[512,8]{0,1:T(8,128)S(1)} all-gather(f32[128,8]{0,1:T(8,128)S(1)} %select_reduce_fusion.1), channel_id=2, replica_groups=mesh['rep'=8,'shard'=4] {'shard'}, dimensions={0}, use_global_device_ids=true | all-gather | bytes 20480 | tf_op jit(solution)/shard_map/all_gather | solution.py:616
  338.0 12.1 fusion.17
  353.6 10.6 convolution_convert_fusion.2
  379.9 86.8 %all-gather.21.cloned.1.call-done = bf16[2,2048,704]{1,2,0:T(8,128)(2,1)} async-done(((bf16[2,512,704]{1,2,0:T(8,128)(2,1)}), bf16[2,2048,704]{1,2,0:T(8,128)(2,1)}) %all-gather.21.cloned.1.call-update) | async-done | bytes 5767184 | tf_op jit(solution)/shard_map/all_gather | solution.py:578
  485.3 40.4 %psum.22 = f32[]{:T(128)} all-reduce(f32[]{:T(128)} %convert_reduce_fusion.1), channel_id=1, replica_groups=mesh['rep'=8,'shard'=4] {'rep','shard'}, use_global_device_ids=true, to_apply=%region_15.16 | all-reduce | flops 1 | bytes 8 | tf_op jit(solution)/shard_map/psum | solution.py:551
  526.5 39.5 %reduce-scatter.13.cloned.1.call-done = bf16[128,2048]{1,0:T(8,128)(2,1)} async-done(((bf16[1024,2048]{1,0:T(8,128)(2,1)}), bf16[128,2048]{1,0:T(8,128)(2,1)}) %reduce-scatter.13.cloned.1.call-update) | async-done | bytes 524304 | tf_op jit(solution)/shard_map/reduce_scatter | solution.py:676
  568.4 46.0 %all-gather.29.cloned.1.call-done = bf16[512,2048]{1,0:T(8,128)(2,1)} async-done(((bf16[128,2048]{1,0:T(8,128)(2,1)}), bf16[512,2048]{1,0:T(8,128)(2,1)}) %all-gather.29.cloned.1.call-update) | async-done | bytes 2097168 | tf_op jit(solution)/shard_map/all_gather | solution.py:616
  622.1 10.3 fusion.95
  632.3 11.8 bitcast_convert_fusion.1
  652.5 10.3 fusion.110
  664.4 11.0 fusion.7
  675.5 23.2 %reduce-scatter.19.cloned.1.call-done = bf16[1,128,2048]{2,1,0:T(8,128)(2,1)} async-done(((bf16[4,128,2048]{2,1,0:T(8,128)(2,1)}), bf16[1,128,2048]{2,1,0:T(8,128)(2,1)}) %reduce-scatter.19.cloned.1.call-update) | async-done | bytes 524304 | tf_op jit(solution)/shard_map/reduce_scatter | solution.py:621
  698.7 54.6 %reduce-scatter.17.cloned.1.call-done = bf16[128,2048]{1,0:T(8,128)(2,1)} async-done(((bf16[1024,2048]{1,0:T(8,128)(2,1)}), bf16[128,2048]{1,0:T(8,128)(2,1)}) %reduce-scatter.17.cloned.1.call-update) | async-done | bytes 524304 | tf_op jit(solution)/shard_map/reduce_scatter | solution.py:724
  764.2 53.0 %all_to_all.43 = bf16[704,8,256]{2,0,1:T(8,128)(2,1)} all-to-all(bf16[704,8,256]{2,0,1:T(8,128)(2,1)S(1)} %bitcast.408), channel_id=1, replica_groups=mesh['rep'=8,'shard'=4] {'rep'}, dimensions={1} | all-to-all | bytes 5767168 | tf_op jit(solution)/shard_map/all_to_all | solution.py:770
  818.5 10.3 convert_bitcast_fusion.1
  861.5 13.8 %convert_bitcast_fusion = bf16[2,2048,1408]{1,2,0:T(8,128)(2,1)} fusion(bf16[640,2048,1]{1,0,2:T(8,128)(2,1)} %bitcast.421, bf16[1,640,1408]{2,1,0:T(8,128)(2,1)} %copy-done.67, bf16[1,640,1408]{2,1,0:T(8,128)(2,1)S(1)} %copy-done.66), kind=kOutput, calls=%fused_computation.7 | convolution fusion | flops 7389544448 | bytes 17760256 | tf_op jit(solution)/shard_map/sd,jsf->jdf/dot_general | solution.py:728
  875.3 11.6 fusion.172
  886.9 10.5 reshape_reshape_squeeze.6
  897.4 15.2 %constant_dynamic-slice_fusion.10 = (bf16[2,1,512,1408]{2,1,0,3:T(2,128)(2,1)}, bf16[2,1,512,1408]{2,1,0,3:T(2,128)(2,1)}) fusion(bf16[2,2,512,1408]{2,1,0,3:T(2,128)(2,1)} %reshape_reshape_squeeze.6, s32[]{:T(128)S(6)} %select_n.223, s32[]{:T(128)S(6)} %select_n.224), kind=kLoop, calls=%fused_computation.255 | loop fusion | bytes 11534344 | tf_op jit(solution)/shard_map/jit(dynamic_index_in_dim)/dynamic_slice | solution.py:494
  912.6 14.2 %copy.201 = bf16[2,1,512,1408]{3,2,0,1:T(8,128)(2,1)} copy(bf16[2,1,512,1408]{2,1,0,3:T(2,128)(2,1)} %get-tuple-element.104) | data formatting | bytes 5767168
  937.4 10.5 reshape_reshape_squeeze.7
  1010.0 14.1 %copy.200 = bf16[2,1,512,1408]{3,2,0,1:T(8,128)(2,1)} copy(bf16[2,1,512,1408]{2,1,0,3:T(2,128)(2,1)} %get-tuple-element.103) | data formatting | bytes 5767168
  1037.4 12.0 all-to-all-done.1
  1067.5 26.6 %collective-permute-done.7 = bf16[2,512,1408]{2,1,0:T(8,128)(2,1)} collective-permute-done((bf16[2,512,1408]{2,1,0:T(8,128)(2,1)}, bf16[2,512,1408]{2,1,0:T(8,128)(2,1)}, u32[]{:S(2)}, u32[]{:S(2)}) %collective-permute-start.7) | collective-permute-done | bytes 2883616 | tf_op jit(solution)/shard_map/ppermute | solution.py:490
  1116.3 24.0 %collective-permute-done.6 = bf16[512,1408]{1,0:T(8,128)(2,1)} collective-permute-done((bf16[512,1408]{1,0:T(8,128)(2,1)}, bf16[512,1408]{1,0:T(8,128)(2,1)}, u32[]{:S(2)}, u32[]{:S(2)}) %collective-permute-start.6) | collective-permute-done | bytes 1441824 | tf_op jit(solution)/shard_map/ppermute | solution.py:490
  1166.6 40.0 %all-reduce = (f32[]{:T(128)}, f32[6,2048]{1,0:T(8,128)S(1)}) all-reduce(f32[]{:T(128)} %multiply_reduce_fusion.7, f32[6,2048]{1,0:T(8,128)S(1)} %pad_maximum_fusion.10), channel_id=1, replica_groups=mesh['rep'=8,'shard'=4] {'rep','shard'}, use_global_device_ids=true, to_apply=%region_13.14 | all-reduce | flops 12289 | bytes 98312 | tf_op jit(solution)/shard_map/psum | solution.py:831
  (347 shorter events, 326.9 us)
Async XLA Ops:
  7.2 83.4 %all-gather.17.cloned.1.call-start = ((), (), s32[]{:S(2)}) async-start(), calls=%async_computation.15 | async-start | bytes 4915200 | tf_op jit(solution)/shard_map/all_gather | solution.py:573
  11.1 143.5 %all-gather.13.cloned.1.call-start = ((), (), s32[]{:S(2)}) async-start(), calls=%async_computation.13 | async-start | bytes 3932160 | tf_op jit(solution)/shard_map/all_gather | solution.py:560
  13.6 178.9 %all-gather.15.cloned.1.call-start = ((), (), s32[]{:S(2)}) async-start(), calls=%async_computation.14 | async-start | bytes 4718592 | tf_op jit(solution)/shard_map/all_gather | solution.py:567
  90.6 123.4 %all-to-all-start = ((bf16[8,120,2048]{2,1,0:T(8,128)(2,1)}), bf16[8,120,2048]{2,1,0:T(8,128)(2,1)}, u32[]{:S(2)}, u32[]{:S(2)}) async-start(bf16[8,120,2048]{2,1,0:T(8,128)(2,1)} %all-gather.17.cloned.1.call-done), calls=%async_computation | async-start | bytes 7864320 | tf_op jit(solution)/shard_map/all_to_all | solution.py:574
  95.1 175.2 %reduce-scatter.11.cloned.1.call-start = ((), (), s32[]{:S(2)}) async-start(), calls=%async_computation.16 | async-start | bytes 4718592 | tf_op jit(solution)/shard_map/reduce_scatter | solution.py:610
  218.8 101.0 %all-gather.27.cloned.1.call-start = ((), (), s32[]{:S(2)}) async-start(), calls=%async_computation.30 | async-start | bytes 2621440 | tf_op jit(solution)/shard_map/all_gather | solution.py:616
  273.7 103.1 %all-gather.19.cloned.1.call-start = ((), (), s32[]{:S(2)}) async-start(), calls=%async_computation.17 | async-start | bytes 4718592 | tf_op jit(solution)/shard_map/all_gather | solution.py:656
  274.3 192.4 %all-gather.21.cloned.1.call-start = ((), (), s32[]{:S(2)}) async-start(), calls=%async_computation.18 | async-start | bytes 7208960 | tf_op jit(solution)/shard_map/all_gather | solution.py:578
  278.1 248.3 %reduce-scatter.15.cloned.1.call-start = ((), (), s32[]{:S(2)}) async-start(), calls=%async_computation.20 | async-start | bytes 2621440 | tf_op jit(solution)/shard_map/reduce_scatter | solution.py:621
  319.8 15.1 %collective-permute-start.1 = (bf16[4,128,2048]{2,1,0:T(8,128)(2,1)}, bf16[4,128,2048]{2,1,0:T(8,128)(2,1)}, u32[]{:S(2)}, u32[]{:S(2)}) collective-permute-start(bf16[4,128,2048]{2,1,0:T(8,128)(2,1)} %bitcast.423), channel_id=1, source_target_pairs={{0,4},{4,0},{8,12},{12,8},{16,20},{20,16},{24,28},{28,24},{1,5},{5... | collective-permute-start | bytes 6291464 | tf_op jit(solution)/shard_map/ppermute | solution.py:490
  372.5 193.5 %reduce-scatter.13.cloned.1.call-start = ((), (), s32[]{:S(2)}) async-start(), calls=%async_computation.19 | async-start | bytes 4718592 | tf_op jit(solution)/shard_map/reduce_scatter | solution.py:676
  484.1 130.3 %all-gather.29.cloned.1.call-start = ((), (), s32[]{:S(2)}) async-start(), calls=%async_computation.31 | async-start | bytes 2621440 | tf_op jit(solution)/shard_map/all_gather | solution.py:616
  568.3 84.2 %all-gather.23.cloned.1.call-start = ((), (), s32[]{:S(2)}) async-start(), calls=%async_computation.21 | async-start | bytes 4718592 | tf_op jit(solution)/shard_map/all_gather | solution.py:690
  614.5 84.2 %reduce-scatter.19.cloned.1.call-start = ((), (), s32[]{:S(2)}) async-start(), calls=%async_computation.23 | async-start | bytes 2621440 | tf_op jit(solution)/shard_map/reduce_scatter | solution.py:621
  652.0 101.3 %reduce-scatter.17.cloned.1.call-start = ((), (), s32[]{:S(2)}) async-start(), calls=%async_computation.22 | async-start | bytes 4718592 | tf_op jit(solution)/shard_map/reduce_scatter | solution.py:724
  675.4 153.6 %all-gather.25.cloned.1.call-start = ((), (), s32[]{:S(2)}) async-start(), calls=%async_computation.24 | async-start | bytes 4718592 | tf_op jit(solution)/shard_map/all_gather | solution.py:780
  758.1 398.8 %reduce-scatter.29.cloned.1.call-start = ((), (), s32[]{:S(2)}) async-start(), calls=%async_computation.29 | async-start | bytes 3604480 | tf_op jit(solution)/shard_map/reduce_scatter | solution.py:771
  817.2 342.1 %reduce-scatter.27.cloned.1.call-start = ((), (), s32[]{:S(2)}) async-start(), calls=%async_computation.28 | async-start | bytes 7208960 | tf_op jit(solution)/shard_map/reduce_scatter | solution.py:765
  828.9 334.2 %reduce-scatter.21.cloned.1.call-start = ((), (), s32[]{:S(2)}) async-start(), calls=%async_computation.25 | async-start | bytes 4718592 | tf_op jit(solution)/shard_map/reduce_scatter | solution.py:819
  926.8 129.4 %collective-permute-start.5 = (bf16[2,512,1408]{2,1,0:T(8,128)(2,1)}, bf16[2,512,1408]{2,1,0:T(8,128)(2,1)}, u32[]{:S(2)}, u32[]{:S(2)}) collective-permute-start(bf16[2,512,1408]{2,1,0:T(8,128)(2,1)} %bitcast.415), channel_id=1, source_target_pairs={{0,8},{4,12},{8,0},{12,4},{16,24},{20,28},{24,16},{28,20},{1,9},{5... | collective-permute-start | bytes 8650760 | tf_op jit(solution)/shard_map/ppermute | solution.py:490
  960.7 71.5 %collective-permute-start.12 = (bf16[704,2,512]{2,0,1:T(8,128)(2,1)}, bf16[704,2,512]{2,0,1:T(8,128)(2,1)S(1)}, u32[]{:S(2)}, u32[]{:S(2)}) collective-permute-start(bf16[704,2,512]{2,0,1:T(8,128)(2,1)} %bitcast.397), channel_id=1, source_target_pairs={{0,16},{4,20},{8,24},{12,28},{16,0},{20,4},{24,8},{28,12},{1,17},{... | collective-permute-start | bytes 4325384 | tf_op jit(solution)/shard_map/ppermute | solution.py:490
  981.3 68.2 %collective-permute-start.10 = (bf16[704,2,512]{2,0,1:T(8,128)(2,1)}, bf16[704,2,512]{2,0,1:T(8,128)(2,1)}, u32[]{:S(2)}, u32[]{:S(2)}) collective-permute-start(bf16[704,2,512]{2,0,1:T(8,128)(2,1)} %bitcast.398), channel_id=1, source_target_pairs={{0,8},{4,12},{8,0},{12,4},{16,24},{20,28},{24,16},{28,20},{1,9},{5... | collective-permute-start | bytes 4325384 | tf_op jit(solution)/shard_map/ppermute | solution.py:490
  987.3 62.2 %all-to-all-start.1 = ((bf16[256,8,256]{2,0,1:T(8,128)(2,1)}), bf16[256,8,256]{2,0,1:T(8,128)(2,1)}, u32[]{:S(2)}, u32[]{:S(2)}) async-start(bf16[256,8,256]{2,0,1:T(8,128)(2,1)} %bitcast.399), calls=%async_computation.8 | async-start | bytes 2097152 | tf_op jit(solution)/shard_map/all_to_all | solution.py:770
  991.5 173.2 %reduce-scatter.25.cloned.1.call-start = ((), (), s32[]{:S(2)}) async-start(), calls=%async_computation.27 | async-start | bytes 1310720 | tf_op jit(solution)/shard_map/reduce_scatter | solution.py:771
  1008.1 86.0 %collective-permute-start.7 = (bf16[2,512,1408]{2,1,0:T(8,128)(2,1)}, bf16[2,512,1408]{2,1,0:T(8,128)(2,1)}, u32[]{:S(2)}, u32[]{:S(2)}) collective-permute-start(bf16[2,512,1408]{2,1,0:T(8,128)(2,1)} %bitcast.418), channel_id=1, source_target_pairs={{0,16},{4,20},{8,24},{12,28},{16,0},{20,4},{24,8},{28,12},{1,17},{... | collective-permute-start | bytes 8650760 | tf_op jit(solution)/shard_map/ppermute | solution.py:490
  1036.0 64.4 %collective-permute-start.13 = (bf16[704,512]{1,0:T(8,128)(2,1)}, bf16[704,512]{1,0:T(8,128)(2,1)}, u32[]{:S(2)}, u32[]{:S(2)}) collective-permute-start(bf16[704,512]{1,0:T(8,128)(2,1)} %dynamic-slice_bitcast_fusion.2), channel_id=1, source_target_pairs={{0,8},{4,12},{8,0},{12,4},{16,24},{20,28},{24,16},{28,20},{1,9},{5... | collective-permute-start | bytes 2162696 | tf_op jit(solution)/shard_map/ppermute | solution.py:490
  1049.5 159.1 %reduce-scatter.23.cloned.1.call-start = ((), (), s32[]{:S(2)}) async-start(), calls=%async_computation.26 | async-start | bytes 3932160 | tf_op jit(solution)/shard_map/reduce_scatter | solution.py:813
  1053.4 56.2 %collective-permute-start.11 = (bf16[704,512]{1,0:T(8,128)(2,1)}, bf16[704,512]{1,0:T(8,128)(2,1)}, u32[]{:S(2)}, u32[]{:S(2)}) collective-permute-start(bf16[704,512]{1,0:T(8,128)(2,1)} %dynamic-slice_bitcast_fusion.3), channel_id=1, source_target_pairs={{0,16},{4,20},{8,24},{12,28},{16,0},{20,4},{24,8},{28,12},{1,17},{... | collective-permute-start | bytes 2162696 | tf_op jit(solution)/shard_map/ppermute | solution.py:490
  1061.7 78.6 %collective-permute-start.6 = (bf16[512,1408]{1,0:T(8,128)(2,1)}, bf16[512,1408]{1,0:T(8,128)(2,1)}, u32[]{:S(2)}, u32[]{:S(2)}) collective-permute-start(bf16[512,1408]{1,0:T(8,128)(2,1)} %dynamic-slice_bitcast_fusion.1), channel_id=1, source_target_pairs={{0,16},{4,20},{8,24},{12,28},{16,0},{20,4},{24,8},{28,12},{1,17},{... | collective-permute-start | bytes 4325384 | tf_op jit(solution)/shard_map/ppermute | solution.py:490
  1098.9 43.2 %collective-permute-start.8 = (bf16[512,1408]{1,0:T(8,128)(2,1)}, bf16[512,1408]{1,0:T(8,128)(2,1)}, u32[]{:S(2)}, u32[]{:S(2)}) collective-permute-start(bf16[512,1408]{1,0:T(8,128)(2,1)} %dynamic-slice_bitcast_fusion), channel_id=1, source_target_pairs={{0,8},{4,12},{8,0},{12,4},{16,24},{20,28},{24,16},{28,20},{1,9},{5... | collective-permute-start | bytes 4325384 | tf_op jit(solution)/shard_map/ppermute | solution.py:490
  1116.3 32.4 %collective-permute-start.14 = (bf16[1408,256]{1,0:T(8,128)(2,1)}, bf16[1408,256]{1,0:T(8,128)(2,1)}, u32[]{:S(2)}, u32[]{:S(2)}) collective-permute-start(bf16[1408,256]{1,0:T(8,128)(2,1)} %bitcast.400), channel_id=1, source_target_pairs={{0,4},{4,0},{8,12},{12,8},{16,20},{20,16},{24,28},{28,24},{1,5},{5... | collective-permute-start | bytes 2162696 | tf_op jit(solution)/shard_map/ppermute | solution.py:490
  1145.0 6.7 collective-permute-start.9
  (72 other events, 925.2 us)
Sparse Core Ops, SparseCore 0:
  11.2 79.2 all-gather.16
  92.7 61.8 all-gather.12
  157.1 35.3 all-gather.14
  218.9 51.3 reduce-scatter.10
  273.8 45.9 all-gather.26
  322.2 35.4 all-gather.18
  359.9 106.6 all-gather.20
  469.1 42.7 reduce-scatter.14
  515.2 50.6 reduce-scatter.12
  568.5 45.9 all-gather.28
  617.1 35.4 all-gather.22
  654.8 43.8 reduce-scatter.18
  702.6 50.6 reduce-scatter.16
  758.2 59.1 all-gather.24
  819.6 57.0 reduce-scatter.28
  878.9 102.0 reduce-scatter.26
  984.6 70.3 reduce-scatter.20
  1057.2 26.4 reduce-scatter.24
  1086.1 58.8 reduce-scatter.22
